TPU v7x, 32 devices: a whole 2x2x4 slice. The times are simulated.
32 devices in a mesh: seq: 8 (over y, x, core), dp: 4 (over z).
Axes of the slice: x: 2, y: 2, z: 4, core: 2. Of those that a mesh axis runs over, the one named last changes fastest.
Arguments:
- queries: bfloat16 [4, 4096, 1024], P('dp', 'seq'), may hold values from -6 to 6
- key_rows: bfloat16 [4, 4096, 1024], P('dp', 'seq'), may hold values from -6 to 6
- value_rows: bfloat16 [4, 4096, 1024], P('dp', 'seq'), may hold values from -6 to 6
- gate_rows: bfloat16 [4, 4096, 1024], P('dp', 'seq'), may hold values from -6 to 6
- cotangent: bfloat16 [4, 4096, 1024], P('dp', 'seq'), may hold values from -6 to 6
- far_blocks: int32 [4, 32, 4], P('dp'), may hold values from 0 to 31, as said below
- treated: int32 [4, 32], P('dp'), may hold values 0 or 1
- norm_gain: float32 [1024], replicated, may hold values from 0.1 to 1.9
- out_weight: bfloat16 [1024, 1024], replicated, may hold values from -0.1875 to 0.1875
Outputs:
- output: bfloat16 [4, 4096, 1024], P('dp', 'seq')
- grad_queries: bfloat16 [4, 4096, 1024], P('dp', 'seq')
- grad_keys: bfloat16 [4, 4096, 1024], P('dp', 'seq')
- grad_values: bfloat16 [4, 4096, 1024], P('dp', 'seq')
- grad_gate: bfloat16 [4, 4096, 1024], P('dp', 'seq')
- grad_weight: float32 [1024, 1024], P(('seq', 'dp'))
- grad_gain: float32 [1024], replicated
Inputs may be any that keep to these rules, and one draw needn't show every extreme that they name: `far_blocks`: every entry names a block of the same history that is held by another index of seq than its query block. Of the 16 entries of the query blocks held by index s of seq, 3 name blocks of index (s + o) mod 8 for o = 1 and o = 2, and 2 for each other o from 3 to 7; which entries these are, and which block of that index, are drawn.
All inputs are finite; a program needn't handle non-finite values. No bound on the sum of `treated` on one device may be relied on, other than what follows from the above.
Results may differ from a plain program's by a relative error of at most 0.0065.
Values may be sent and summed in bfloat16 or wider, within the bound.
A program may use at most 192 MiB of HBM per device.

v0:
```python
import jax
import jax.numpy as jnp
from jax import lax
from jax.sharding import PartitionSpec as P

HEADS = 8
HEAD_DIM = 128
BLK = 128
FAR = 4
epsilon = 1e-05


def from_behind(value, axis, by):
    peers = lax.axis_size(axis)
    pairs = [(i, i + by) for i in range(peers) if 0 <= i + by < peers]
    return lax.ppermute(value, axis, pairs)


def to_heads(rows):
    return rows.reshape(rows.shape[:-1] + (HEADS, rows.shape[-1] // HEADS))


def as_bf16(values):
    return values.astype(jnp.bfloat16)


def pair_scores(query_part, key_part):
    scores = jnp.einsum(
        "pqhd,pkhd->phqk",
        to_heads(query_part),
        to_heads(key_part),
        preferred_element_type=jnp.float32,
    )
    return scores * HEAD_DIM ** (-0.5)


def pair_forward(query_part, key_part, value_part, pair_mask):
    weights = as_bf16(jax.nn.silu(pair_scores(query_part, key_part)) * pair_mask[:, None])
    result = jnp.einsum(
        "phqk,pkhd->pqhd", weights, to_heads(value_part), preferred_element_type=jnp.float32
    )
    return result.reshape(query_part.shape)


def pair_backward(query_part, key_part, value_part, grad_part, pair_mask):
    scores = pair_scores(query_part, key_part)
    logistic = jax.nn.sigmoid(scores)
    weights = as_bf16(jax.nn.silu(scores) * pair_mask[:, None])
    grad_heads = to_heads(grad_part)
    grad_weights = jnp.einsum(
        "pqhd,pkhd->phqk", grad_heads, to_heads(value_part), preferred_element_type=jnp.float32
    )
    grad_value = jnp.einsum(
        "phqk,pqhd->pkhd", weights, grad_heads, preferred_element_type=jnp.float32
    )
    grad_scores = as_bf16(
        grad_weights
        * logistic
        * (1.0 + scores * (1.0 - logistic))
        * pair_mask[:, None]
        * HEAD_DIM ** (-0.5)
    )
    grad_query = jnp.einsum(
        "phqk,pkhd->pqhd", grad_scores, to_heads(key_part), preferred_element_type=jnp.float32
    )
    grad_key = jnp.einsum(
        "phqk,pqhd->pkhd", grad_scores, to_heads(query_part), preferred_element_type=jnp.float32
    )
    row_shape = query_part.shape
    return (
        grad_query.reshape(row_shape),
        grad_key.reshape(row_shape),
        grad_value.reshape(row_shape),
    )


def far_plan(far_all, my_index, seq_count, blocks, capacity):
    block_ids = far_all.reshape(seq_count, blocks * FAR)
    owners = block_ids // blocks
    local_ids = block_ids % blocks
    positions = jnp.arange(blocks * FAR)
    same_owner = owners[:, :, None] == owners[:, None, :]
    before = positions[None, :] < positions[:, None]
    slot_rank = jnp.sum(same_owner & before[None], axis=2)
    slot_ids = jnp.arange(capacity)
    send_hit = (owners[:, None, :] == my_index) & (slot_rank[:, None, :] == slot_ids[None, :, None])
    all_local = jnp.sum(jnp.where(send_hit, local_ids[:, None, :], 0), axis=2).reshape(-1)
    all_ok = jnp.any(send_hit, axis=2).reshape(-1)
    my_owners = lax.dynamic_index_in_dim(owners, my_index, 0, keepdims=False)
    my_ranks = lax.dynamic_index_in_dim(slot_rank, my_index, 0, keepdims=False)
    slot_count = seq_count * capacity
    read_at = my_owners * capacity + my_ranks
    back_hit = read_at[None, :] == jnp.arange(slot_count)[:, None]
    return (all_local, all_ok, read_at, back_hit)


def body(
    queries, key_rows, value_rows, gate_rows, cotangent, far_blocks, treated, norm_gain, out_weight
):
    width = queries.shape[2]
    blocks = queries.shape[1] // BLK
    seq_count = lax.axis_size("seq")
    my_index = lax.axis_index("seq")
    requests = blocks * FAR
    capacity = (requests + seq_count - 2) // (seq_count - 1)
    slot_count = seq_count * capacity
    query_blocks = queries[0].reshape(blocks, BLK, width)
    key_blocks = key_rows[0].reshape(blocks, BLK, width)
    value_blocks = value_rows[0].reshape(blocks, BLK, width)
    both_blocks = jnp.concatenate([key_blocks, value_blocks], axis=2)
    from_prev = from_behind(both_blocks[blocks - 1], "seq", 1)
    prev_both = jnp.concatenate([from_prev[None], both_blocks[:-1]], axis=0)
    prev_keys = prev_both[:, :, :width]
    prev_values = prev_both[:, :, width:]
    causal = jnp.tril(jnp.ones((BLK, BLK), jnp.float32))[None]
    all_ones = jnp.ones((1, BLK, BLK), jnp.float32)
    all_local, all_ok, read_at, back_hit = far_plan(
        far_blocks[0], my_index, seq_count, blocks, capacity
    )
    block_ids = lax.dynamic_slice_in_dim(far_blocks[0], my_index * blocks, blocks, 0).reshape(
        requests
    )
    far_mask = treated[0][block_ids].astype(jnp.float32)[:, None, None]
    far_queries = jnp.repeat(query_blocks, FAR, axis=0)
    back_matrix = back_hit.astype(jnp.bfloat16)
    local_onehot = ((all_local[None, :] == jnp.arange(blocks)[:, None]) & all_ok[None, :]).astype(
        jnp.bfloat16
    )
    diag_out = pair_forward(query_blocks, key_blocks, value_blocks, causal)
    prev_out = pair_forward(query_blocks, prev_keys, prev_values, all_ones)
    send_both = jnp.where(
        all_ok[:, None, None], both_blocks[all_local], jnp.zeros((), jnp.bfloat16)
    )
    got_both = lax.all_to_all(
        send_both.reshape(seq_count, capacity, BLK, 2 * width),
        "seq",
        split_axis=0,
        concat_axis=0,
        tiled=True,
    )
    received = got_both.reshape(slot_count, BLK, 2 * width)
    far_both = received[read_at]
    far_keys = far_both[:, :, :width]
    far_values = far_both[:, :, width:]
    far_terms = as_bf16(pair_forward(far_queries, far_keys, far_values, far_mask))
    far_sum = (
        lax.optimization_barrier(far_terms)
        .astype(jnp.float32)
        .reshape(blocks, FAR, BLK, width)
        .sum(axis=1)
    )
    attention = (diag_out + prev_out + far_sum).reshape(blocks * BLK, width)
    centered = attention - jnp.mean(attention, axis=1, keepdims=True)
    inv_std = lax.rsqrt(jnp.mean(centered * centered, axis=1, keepdims=True) + epsilon)
    normed = centered * inv_std
    gate_vals = gate_rows[0].astype(jnp.float32)
    mixed = as_bf16(normed * norm_gain * gate_vals)
    output = jnp.dot(mixed, out_weight, preferred_element_type=jnp.float32).astype(jnp.bfloat16)
    grad_in = cotangent[0]
    grad_mixed = lax.dot_general(
        grad_in, out_weight, (((1,), (1,)), ((), ())), preferred_element_type=jnp.float32
    )
    grad_weight = lax.psum_scatter(
        lax.dot_general(
            mixed, grad_in, (((0,), (0,)), ((), ())), preferred_element_type=jnp.float32
        ),
        ("seq", "dp"),
        scatter_dimension=0,
        tiled=True,
    )
    grad_gate = as_bf16(grad_mixed * normed * norm_gain)
    scaled = grad_mixed * gate_vals
    grad_gain = lax.psum(jnp.sum(scaled * normed, axis=0), ("seq", "dp"))
    grad_hat = scaled * norm_gain
    grad_attn = inv_std * (
        grad_hat
        - jnp.mean(grad_hat, axis=1, keepdims=True)
        - normed * jnp.mean(grad_hat * normed, axis=1, keepdims=True)
    )
    grad_blocks = as_bf16(grad_attn).reshape(blocks, BLK, width)
    dq_diag, dk_diag, dv_diag = pair_backward(
        query_blocks, key_blocks, value_blocks, grad_blocks, causal
    )
    dq_prev, dk_prev, dv_prev = pair_backward(
        query_blocks, prev_keys, prev_values, grad_blocks, all_ones
    )
    prev_terms = lax.optimization_barrier(as_bf16(jnp.concatenate([dk_prev, dv_prev], axis=2)))
    from_next = from_behind(prev_terms[0], "seq", -1)
    next_terms = jnp.concatenate([prev_terms[1:], from_next[None]], axis=0).astype(jnp.float32)
    far_grads = jnp.repeat(grad_blocks, FAR, axis=0)
    dq_far, dk_far, dv_far = pair_backward(far_queries, far_keys, far_values, far_grads, far_mask)
    query_terms = as_bf16(dq_far)
    back_terms = as_bf16(jnp.concatenate([dk_far, dv_far], axis=2))
    send_back = jnp.dot(
        back_matrix, back_terms.reshape(requests, -1), preferred_element_type=jnp.float32
    )
    send_back = as_bf16(send_back).reshape(slot_count, BLK, 2 * width)
    got_back = lax.all_to_all(
        send_back.reshape(seq_count, capacity, BLK, 2 * width),
        "seq",
        split_axis=0,
        concat_axis=0,
        tiled=True,
    )
    owned_terms = got_back.reshape(slot_count, BLK * 2 * width)
    far_query = (
        lax.optimization_barrier(query_terms)
        .astype(jnp.float32)
        .reshape(blocks, FAR, BLK, width)
        .sum(axis=1)
    )
    owned_sum = jnp.dot(
        local_onehot, lax.optimization_barrier(owned_terms), preferred_element_type=jnp.float32
    )
    owned_sum = owned_sum.reshape(blocks, BLK, 2 * width)
    rows = blocks * BLK
    grad_queries = as_bf16(dq_diag + dq_prev + far_query).reshape(1, rows, width)
    key_total = jnp.concatenate([dk_diag, dv_diag], axis=2) + next_terms + owned_sum
    grad_keys = as_bf16(key_total[:, :, :width]).reshape(1, rows, width)
    grad_values = as_bf16(key_total[:, :, width:]).reshape(1, rows, width)
    return (
        output[None],
        grad_queries,
        grad_keys,
        grad_values,
        grad_gate[None],
        grad_weight,
        grad_gain,
    )


def solution(mesh):
    in_specs = (
        P("dp", "seq", None),
        P("dp", "seq", None),
        P("dp", "seq", None),
        P("dp", "seq", None),
        P("dp", "seq", None),
        P("dp", None, None),
        P("dp", None),
        P(),
        P(),
    )
    out_specs = (
        P("dp", "seq", None),
        P("dp", "seq", None),
        P("dp", "seq", None),
        P("dp", "seq", None),
        P("dp", "seq", None),
        P(("seq", "dp"), None),
        P(),
    )
    return jax.shard_map(body, mesh=mesh, in_specs=in_specs, out_specs=out_specs, check_vma=False)
```

profile of v0, /device:TPU:0, one launch (start us, length us, event | category | flops | bytes accessed | tf_op | source)
XLA Modules:
  0.0 594.2 jit_solution(34854243904092478)
XLA Ops:
  12.2 7.5 %gather_fusion = bf16[24,128,2048]{2,1,0:T(8,128)(2,1)} fusion(bf16[4,128,2048]{2,1,0:T(8,128)(2,1)} %pad_maximum_fusion.1, s32[1024]{0:T(1024)S(1)} %pad_clamp_fusion.2), kind=kCustom, calls=%fused_computation | custom fusion | bytes 25165920 | tf_op jit(solution)/shard_map/gather | solution.py:132
  19.7 10.6 %broadcast_select_fusion = bf16[8,3,128,2048]{3,2,1,0:T(8,128)(2,1)} fusion(bf16[8,3,128,2048]{3,2,1,0:T(8,128)(2,1)} %bitcast.251, pred[8,3]{1,0:T(8,128)(4,1)S(1)} %copy.282), kind=kLoop, calls=%fused_computation.4 | loop fusion | flops 6291456 | bytes 25165848 | tf_op jit(solution)/shard_map/jit(_where)/select_n | solution.py:131
  30.3 5.5 all-to-all-start
  73.0 102.6 %all-to-all-done = bf16[8,3,128,2048]{3,2,1,0:T(8,128)(2,1)} async-done(((bf16[8,3,128,2048]{3,2,1,0:T(8,128)(2,1)}), bf16[8,3,128,2048]{3,2,1,0:T(8,128)(2,1)}, u32[]{:S(2)}, u32[]{:S(2)}) %all-to-all-start) | async-done | bytes 12582944 | tf_op jit(solution)/shard_map/all_to_all | solution.py:134
  175.6 9.5 %gather_fusion.1 = bf16[16,128,2048]{2,1,0:T(8,128)(2,1)} fusion(bf16[24,128,2048]{2,1,0:T(8,128)(2,1)} %bitcast.11, s32[1024]{0:T(1024)S(1)} %pad_clamp_fusion.1), kind=kCustom, calls=%fused_computation.1 | custom fusion | bytes 16777280 | tf_op jit(solution)/shard_map/gather | solution.py:142
  185.1 6.1 %fusion.73 = (bf16[16,128,1024]{2,1,0:T(8,128)(2,1)}, bf16[16,128,1024]{2,1,0:T(8,128)(2,1)}) fusion(bf16[16,128,2048]{2,1,0:T(8,128)(2,1)} %gather_fusion.1), kind=kLoop, calls=%fused_computation.143 | loop fusion | bytes 16777216 | tf_op jit(solution)/shard_map/slice | solution.py:143
  191.1 6.4 %copy.285 = bf16[16,128,1024]{1,2,0:T(8,128)(2,1)} copy(bf16[16,128,1024]{2,1,0:T(8,128)(2,1)} %get-tuple-element.18) | data formatting | bytes 8388608 | tf_op jit(solution)/shard_map/slice | solution.py:143
  197.6 6.3 %copy.284 = bf16[16,128,1024]{1,2,0:T(8,128)(2,1)} copy(bf16[16,128,1024]{2,1,0:T(8,128)(2,1)} %get-tuple-element.19) | data formatting | bytes 8388608 | tf_op jit(solution)/shard_map/slice | solution.py:144
  206.3 5.6 fusion.4
  219.0 5.4 fusion.71
  239.8 5.0 convolution_convert_fusion.1
  244.8 12.7 %fusion.9 = bf16[16,8,128,128]{2,3,1,0:T(8,128)(2,1)} fusion(f32[16,8,128,128]{3,2,1,0:T(8,128)} %get-tuple-element.29, f32[16]{0:T(128)S(1)} %convert_element_type.121, bf16[16,128,8,128]{1,3,2,0:T(8,128)(2,1)} %bitcast.258, bf16[16,128,8,128]{1,3,2,0:T(8,128)(2,1)} %bitcast.261), kind=kOutput, calls=%fused_computation.20 | convolution fusion | flops 562036736 | bytes 20971584 | tf_op jit(solution)/shard_map/pqhd,pkhd->phqk/dot_general | solution.py:50
  257.4 6.7 %copy.315 = bf16[16,128,1024]{2,1,0:T(8,128)(2,1)} copy(bf16[16,128,1024]{1,2,0:T(8,128)(2,1)} %bitcast.263) | data formatting | bytes 8388608 | tf_op jit(solution)/shard_map/reshape | solution.py:73
  264.1 8.4 %convolution_convert_fusion.2 = bf16[16,8,128,128]{2,3,1,0:T(8,128)(2,1)} fusion(bf16[16,8,128,128]{2,3,1,0:T(8,128)(2,1)} %fusion.9, bf16[16,128,8,128]{1,3,2,0:T(8,128)(2,1)} %bitcast.256), kind=kOutput, calls=%fused_computation.26 | convolution fusion | flops 538968064 | bytes 12582912 | tf_op jit(solution)/shard_map/phqk,pqhd->pkhd/dot_general | solution.py:66
  272.5 6.4 %copy.314 = bf16[16,128,1024]{2,1,0:T(8,128)(2,1)} copy(bf16[16,128,1024]{1,2,0:T(8,128)(2,1)} %bitcast.265) | data formatting | bytes 8388608 | tf_op jit(solution)/shard_map/reshape | solution.py:72
  279.0 8.3 %pad_maximum_fusion = bf16[16,128,2048]{2,1,0:T(8,128)(2,1)} fusion(bf16[16,128,1024]{2,1,0:T(8,128)(2,1)} %copy.315, bf16[16,128,1024]{2,1,0:T(8,128)(2,1)} %copy.314), kind=kLoop, calls=%fused_computation.5 | loop fusion | flops 16777216 | bytes 16777216 | tf_op jit(solution)/shard_map/concatenate | solution.py:193
  287.3 11.3 %copy.339 = bf16[2,8,128,2048]{3,1,2,0:T(8,128)(2,1)} copy(bf16[2,8,128,2048]{3,2,1,0:T(8,128)(2,1)} %bitcast.252) | data formatting | bytes 16777216
  298.6 11.4 %convolution_convert_fusion = bf16[24,262144]{1,0:T(8,128)(2,1)} fusion(bf16[16,262144]{1,0:T(8,128)(2,1)} %bitcast.249, s32[16]{0:T(128)S(1)} %bitcast.300), kind=kOutput, calls=%fused_computation.3 | convolution fusion | flops 207618432 | bytes 20971584 | tf_op jit(solution)/shard_map/dot_general | solution.py:194
  309.9 14.7 %copy.340 = bf16[3,8,128,2048]{3,2,1,0:T(8,128)(2,1)} copy(bf16[3,8,128,2048]{3,1,2,0:T(8,128)(2,1)} %bitcast.247) | data formatting | bytes 25165824
  324.6 17.8 %all-to-all-start.1 = ((bf16[8,3,128,2048]{3,2,1,0:T(8,128)(2,1)}), bf16[8,3,128,2048]{3,2,1,0:T(8,128)(2,1)}, u32[]{:S(2)}, u32[]{:S(2)}) async-start(bf16[8,3,128,2048]{3,2,1,0:T(8,128)(2,1)} %bitcast.250), calls=%async_computation.1 | async-start | bytes 25165824 | tf_op jit(solution)/shard_map/all_to_all | solution.py:198
  351.6 4.9 fusion.34
  395.8 147.2 %psum.7 = f32[1024]{0:T(1024)} all-reduce(f32[1024]{0:T(1024)S(1)} %get-tuple-element.7), channel_id=1, replica_groups=mesh['seq'=8,'dp'=4] {'seq','dp'}, use_global_device_ids=true, to_apply=%region_11.12 | all-reduce | flops 1024 | bytes 8192 | tf_op jit(solution)/shard_map/psum | solution.py:173
  552.9 11.7 %copy.341 = bf16[3,8,128,2048]{3,1,2,0:T(8,128)(2,1)S(1)} copy(bf16[3,8,128,2048]{3,2,1,0:T(8,128)(2,1)} %bitcast.95) | data formatting | bytes 25165824
  572.3 5.4 copy.316
  (157 shorter events, 142.2 us)
Async XLA Ops:
  7.2 43.2 %copy-start = (bf16[1024,1024]{1,0:T(8,128)(2,1)S(1)}, bf16[1024,1024]{1,0:T(8,128)(2,1)}, u32[]{:S(2)}) copy-start(bf16[1024,1024]{1,0:T(8,128)(2,1)} %param.17) | copy-start | bytes 6291460
  9.0 3.2 copy-start.30
  30.3 5.5 copy-start.11
  30.3 145.3 %all-to-all-start = ((bf16[8,3,128,2048]{3,2,1,0:T(8,128)(2,1)}), bf16[8,3,128,2048]{3,2,1,0:T(8,128)(2,1)}, u32[]{:S(2)}, u32[]{:S(2)}) async-start(bf16[8,3,128,2048]{3,2,1,0:T(8,128)(2,1)} %broadcast_select_fusion), calls=%async_computation | async-start | bytes 25165824 | tf_op jit(solution)/shard_map/all_to_all | solution.py:134
  35.8 5.0 copy-start.32
  37.6 25.2 %collective-permute-start = (bf16[128,2048]{1,0:T(8,128)(2,1)}, bf16[128,2048]{1,0:T(8,128)(2,1)}, u32[]{:S(2)}, u32[]{:S(2)}) collective-permute-start(bf16[128,2048]{1,0:T(8,128)(2,1)} %fusion.48), channel_id=1, source_target_pairs={{0,4},{4,8},{8,12},{12,16},{16,20},{20,24},{24,28},{1,5},{5,9},{9,... | collective-permute-start | bytes 1572872 | tf_op jit(solution)/shard_map/ppermute | solution.py:16
  45.3 2.8 copy-start.14
  50.4 2.6 copy-start.1
  58.4 4.4 copy-start.19
  203.8 2.5 copy-start.9
  206.0 5.9 copy-start.7
  206.3 5.6 copy-start.10
  224.6 2.9 copy-start.29
  227.5 4.6 copy-start.4
  227.5 4.6 copy-start.12
  237.3 2.5 copy-start.6
  239.4 5.3 copy-start.8
  324.6 228.2 %all-to-all-start.1 = ((bf16[8,3,128,2048]{3,2,1,0:T(8,128)(2,1)}), bf16[8,3,128,2048]{3,2,1,0:T(8,128)(2,1)}, u32[]{:S(2)}, u32[]{:S(2)}) async-start(bf16[8,3,128,2048]{3,2,1,0:T(8,128)(2,1)} %bitcast.250), calls=%async_computation.1 | async-start | bytes 25165824 | tf_op jit(solution)/shard_map/all_to_all | solution.py:198
  342.4 244.6 %reduce-scatter.2.cloned.1.call-start = ((), (), s32[]{:S(2)}) async-start(), calls=%async_computation.3 | async-start | bytes 4325376 | tf_op jit(solution)/shard_map/reduce_scatter | solution.py:163
  368.3 2.3 copy-start.22
  368.3 2.6 copy-start.25
  384.6 193.1 %collective-permute-start.1 = (bf16[128,2048]{0,1:T(8,128)(2,1)}, bf16[128,2048]{0,1:T(8,128)(2,1)}, u32[]{:S(2)}, u32[]{:S(2)}) collective-permute-start(bf16[128,2048]{0,1:T(8,128)(2,1)} %slice_bitcast_fusion), channel_id=1, source_target_pairs={{4,0},{8,4},{12,8},{16,12},{20,16},{24,20},{28,24},{5,1},{9,5},{13... | collective-permute-start | bytes 1572872 | tf_op jit(solution)/shard_map/ppermute | solution.py:16
  543.0 3.1 copy-start.17
  543.0 3.1 copy-start.18
  (14 other events, 23.7 us)
Sparse Core Ops, SparseCore 0:
  356.6 152.8 reduce-scatter.1
where the time goes:
time: 606 us; the launch traced here: 594 us
  local copies, waits for them, and re-layouts  159 us (26%)
  blocking collectives  147 us (24%)
  waiting for transfers between devices  103 us (17%)
  matrix products  89.9 us (15%)
  other arithmetic  52.6 us (9%)
  starting transfers between devices  27.9 us (5%)
  between operations  14.8 us (2%)
    psum x1, blocking collectives, body(): grad_gain = lax.psum(jnp.sum(scaled * normed, axis=0), ('seq', 'dp'))  147 us
    all_to_all x1, waiting for transfers between devices, body(): lax.all_to_all(send_both.reshape(seq_count, capacity, BLK, 2 * width), 's...  103 us
    unnamed x75, local copies, waits for them, and re-layouts  57.6 us
    all_to_all x1, starting transfers between devices, body(): lax.all_to_all(send_back.reshape(seq_count, capacity, BLK, 2 * width), 's...  17.8 us
    dot_general x3, matrix products, pair_backward(): jnp.einsum('pqhd,pkhd->phqk', grad_heads, to_heads(value_part), preferred...  17.5 us
    slice x2, local copies, waits for them, and re-layouts, body(): far_keys = far_both[:, :, :width]  12.5 us
  transfers between devices with their start and end apart: 5, of which 1 were waited for; matrix products, arithmetic and copies ran while one was open for 21% of the time, Pallas kernels for 0%

commit v1 on v0

--- a/solution.py
+++ b/solution.py
@@ -131,13 +131,20 @@
     send_both = jnp.where(
         all_ok[:, None, None], both_blocks[all_local], jnp.zeros((), jnp.bfloat16)
     )
-    got_both = lax.all_to_all(
-        send_both.reshape(seq_count, capacity, BLK, 2 * width),
-        "seq",
-        split_axis=0,
-        concat_axis=0,
-        tiled=True,
-    )
+    x = send_both.reshape(seq_count, capacity, BLK, 2 * width)
+    ways, here = (lax.axis_size("seq"), lax.axis_index("seq"))
+    width_2 = x.shape[0] // ways
+    shape = list(x.shape)
+    shape[0] = width_2
+    height = shape[0]
+    shape[0] = height * ways
+    full = jnp.zeros(shape, x.dtype)
+    for mask in range(ways):
+        part = lax.dynamic_slice_in_dim(x, (here ^ mask) * width_2, width_2, axis=0)
+        if mask:
+            part = lax.ppermute(part, "seq", [(d, d ^ mask) for d in range(ways)])
+        full = lax.dynamic_update_slice_in_dim(full, part, (here ^ mask) * height, axis=0)
+    got_both = full
     received = got_both.reshape(slot_count, BLK, 2 * width)
     far_both = received[read_at]
     far_keys = far_both[:, :, :width]

time: 606 us -> 641 us (1.058); the launches traced: 594 us -> 636 us
  starting transfers between devices: 27.9 us -> 70.7 us
  local copies, waits for them, and re-layouts: 159 us -> 188 us
  waiting for transfers between devices: 103 us -> 74.3 us
    all_to_all x1 -> x0, waiting for transfers between devices: 103 us -> none  [body(): lax.all_to_all(send_both.reshape(seq_count, capacity, BLK, 2 * width), 's...]
    ppermute x0 -> x7, waiting for transfers between devices: none -> 74.3 us  [body(): part = lax.ppermute(part, 'seq', [(d, d ^ mask) for d in range(ways)])]
    ppermute x0 -> x7, starting transfers between devices: none -> 60.8 us  [body(): part = lax.ppermute(part, 'seq', [(d, d ^ mask) for d in range(ways)])]
    dynamic_update_slice x0 -> x7, local copies, waits for them, and re-layouts: none -> 16.4 us  [body(): lax.dynamic_update_slice_in_dim(full, part, (here ^ mask) * height, axis=0)]
    all_to_all x1, starting transfers between devices: 17.8 us -> 5.34 us  [body(): lax.all_to_all(send_back.reshape(seq_count, capacity, BLK, 2 * width), 's...]
    dynamic_slice x0 -> x1, local copies, waits for them, and re-layouts: none -> 8.56 us  [body(): part = lax.dynamic_slice_in_dim(x, (here ^ mask) * width_2, width_2, axis=0)]
    unnamed x75 -> x85, local copies, waits for them, and re-layouts: 57.6 us -> 57.6 us
  transfers between devices with their start and end apart: 5 -> 11, of which waited for: 1 -> 1; matrix products, arithmetic and copies ran while one was open for 21% -> 21% of each run, Pallas kernels for 0% -> 0%
where the time goes in v1:
time: 641 us; the launch traced here: 636 us
  local copies, waits for them, and re-layouts  188 us (29%)
  blocking collectives  151 us (24%)
  matrix products  86.8 us (14%)
  waiting for transfers between devices  74.3 us (12%)
  starting transfers between devices  70.7 us (11%)
  other arithmetic  50.5 us (8%)
  between operations  15 us (2%)
    psum x1, blocking collectives, body(): grad_gain = lax.psum(jnp.sum(scaled * normed, axis=0), ('seq', 'dp'))  151 us
    ppermute x7, waiting for transfers between devices, body(): part = lax.ppermute(part, 'seq', [(d, d ^ mask) for d in range(ways)])  74.3 us
    ppermute x7, starting transfers between devices, body(): part = lax.ppermute(part, 'seq', [(d, d ^ mask) for d in range(ways)])  60.8 us
    unnamed x85, local copies, waits for them, and re-layouts  57.6 us
    dot_general x3, matrix products, pair_backward(): jnp.einsum('pqhd,pkhd->phqk', grad_heads, to_heads(value_part), preferred...  19.8 us
    dynamic_update_slice x7, local copies, waits for them, and re-layouts, body(): lax.dynamic_update_slice_in_dim(full, part, (here ^ mask) * height, axis=0)  16.4 us
  transfers between devices with their start and end apart: 11, of which 1 were waited for; matrix products, arithmetic and copies ran while one was open for 21% of the time, Pallas kernels for 0%

profile of v1, /device:TPU:0, one launch (start us, length us, event | category | flops | bytes accessed | tf_op | source)
XLA Modules:
  0.0 636.2 jit_solution(15918458322780536137)
XLA Ops:
  12.2 7.5 %gather_fusion = bf16[24,128,2048]{2,1,0:T(8,128)(2,1)} fusion(bf16[4,128,2048]{2,1,0:T(8,128)(2,1)} %pad_maximum_fusion.1, s32[1024]{0:T(1024)S(1)} %pad_clamp_fusion.2), kind=kCustom, calls=%fused_computation | custom fusion | bytes 25165920 | tf_op jit(solution)/shard_map/gather | solution.py:132
  19.7 10.7 %broadcast_select_fusion = bf16[8,3,128,2048]{3,2,1,0:T(8,128)(2,1)} fusion(bf16[8,3,128,2048]{3,2,1,0:T(8,128)(2,1)} %bitcast.251, pred[8,3]{1,0:T(8,128)(4,1)S(1)} %copy.282), kind=kLoop, calls=%fused_computation.4 | loop fusion | flops 6291456 | bytes 25165848 | tf_op jit(solution)/shard_map/jit(_where)/select_n | solution.py:131
  30.4 6.1 broadcast_in_dim.45
  36.5 8.6 %constant_dynamic-slice_fusion.2 = (bf16[1,3,128,2048]{3,2,1,0:T(8,128)(2,1)}, bf16[1,3,128,2048]{3,2,1,0:T(8,128)(2,1)}, bf16[1,3,128,2048]{3,2,1,0:T(8,128)(2,...) fusion(bf16[8,3,128,2048]{3,2,1,0:T(8,128)(2,1)} %broadcast_sel, ...), kind=kLoop, calls=%fused_computation.116 | loop fusion | bytes 25165856 | tf_op jit(solution)/shard_map/dynamic_slice | solution.py:143
  71.0 52.4 %collective-permute-start.5 = (bf16[1,3,128,2048]{3,2,1,0:T(8,128)(2,1)}, bf16[1,3,128,2048]{3,2,1,0:T(8,128)(2,1)}, u32[]{:S(2)}, u32[]{:S(2)}) collective-permute-start(bf16[1,3,128,2048]{3,2,1,0:T(8,128)(2,1)} %get-tuple-element.20), channel_id=1, source_target_pairs={{0,20},{4,16},{8,28},{12,24},{16,4},{20,0},{24,12},{28,8},{1,21},{... | collective-permute-start | bytes 4718600 | tf_op jit(solution)/shard_map/ppermute | solution.py:145
  151.4 74.2 %collective-permute-done.5 = bf16[1,3,128,2048]{3,2,1,0:T(8,128)(2,1)} collective-permute-done((bf16[1,3,128,2048]{3,2,1,0:T(8,128)(2,1)}, bf16[1,3,128,2048]{3,2,1,0:T(8,128)(2,1)}, u32[]{:S(2)}, u32[]{:S(2)}) %collective-permute-start.5) | collective-permute-done | bytes 1572896 | tf_op jit(solution)/shard_map/ppermute | solution.py:145
  231.1 9.4 %gather_fusion.1 = bf16[16,128,2048]{2,1,0:T(8,128)(2,1)} fusion(bf16[24,128,2048]{2,1,0:T(8,128)(2,1)} %bitcast.252, s32[1024]{0:T(1024)S(1)} %pad_clamp_fusion.1), kind=kCustom, calls=%fused_computation.1 | custom fusion | bytes 16777280 | tf_op jit(solution)/shard_map/gather | solution.py:149
  240.5 6.1 fusion.73
  246.6 6.4 %copy.285 = bf16[16,128,1024]{1,2,0:T(8,128)(2,1)} copy(bf16[16,128,1024]{2,1,0:T(8,128)(2,1)} %get-tuple-element.26) | data formatting | bytes 8388608 | tf_op jit(solution)/shard_map/slice | solution.py:150
  252.9 6.3 copy.284
  261.7 5.8 fusion.4
  274.4 5.4 fusion.71
  300.2 6.8 %copy.315 = bf16[16,128,1024]{2,1,0:T(8,128)(2,1)} copy(bf16[16,128,1024]{1,2,0:T(8,128)(2,1)} %bitcast.265) | data formatting | bytes 8388608 | tf_op jit(solution)/shard_map/reshape | solution.py:73
  307.0 12.7 %fusion.9 = bf16[16,8,128,128]{2,3,1,0:T(8,128)(2,1)} fusion(f32[16,8,128,128]{3,2,1,0:T(8,128)} %get-tuple-element.37, f32[16]{0:T(128)S(1)} %convert_element_type.121, bf16[16,128,8,128]{1,3,2,0:T(8,128)(2,1)} %bitcast.259, bf16[16,128,8,128]{1,3,2,0:T(8,128)(2,1)} %bitcast.262), kind=kOutput, calls=%fused_computation.20 | convolution fusion | flops 562036736 | bytes 20971584 | tf_op jit(solution)/shard_map/pqhd,pkhd->phqk/dot_general | solution.py:50
  319.7 8.4 %convolution_convert_fusion.2 = bf16[16,8,128,128]{2,3,1,0:T(8,128)(2,1)} fusion(bf16[16,8,128,128]{2,3,1,0:T(8,128)(2,1)} %fusion.9, bf16[16,128,8,128]{1,3,2,0:T(8,128)(2,1)} %bitcast.257), kind=kOutput, calls=%fused_computation.26 | convolution fusion | flops 538968064 | bytes 12582912 | tf_op jit(solution)/shard_map/phqk,pqhd->pkhd/dot_general | solution.py:66
  328.2 6.4 %copy.314 = bf16[16,128,1024]{2,1,0:T(8,128)(2,1)} copy(bf16[16,128,1024]{1,2,0:T(8,128)(2,1)} %bitcast.266) | data formatting | bytes 8388608 | tf_op jit(solution)/shard_map/reshape | solution.py:72
  334.6 8.2 %pad_maximum_fusion = bf16[16,128,2048]{2,1,0:T(8,128)(2,1)} fusion(bf16[16,128,1024]{2,1,0:T(8,128)(2,1)} %copy.315, bf16[16,128,1024]{2,1,0:T(8,128)(2,1)} %copy.314), kind=kLoop, calls=%fused_computation.5 | loop fusion | flops 16777216 | bytes 16777216 | tf_op jit(solution)/shard_map/concatenate | solution.py:200
  342.8 11.2 %copy.339 = bf16[2,8,128,2048]{3,1,2,0:T(8,128)(2,1)} copy(bf16[2,8,128,2048]{3,2,1,0:T(8,128)(2,1)} %bitcast.253) | data formatting | bytes 16777216
  354.1 11.3 %convolution_convert_fusion = bf16[24,262144]{1,0:T(8,128)(2,1)} fusion(bf16[16,262144]{1,0:T(8,128)(2,1)} %bitcast.249, s32[16]{0:T(128)S(1)} %bitcast.301), kind=kOutput, calls=%fused_computation.3 | convolution fusion | flops 207618432 | bytes 20971584 | tf_op jit(solution)/shard_map/dot_general | solution.py:201
  365.4 14.5 %copy.340 = bf16[3,8,128,2048]{3,2,1,0:T(8,128)(2,1)} copy(bf16[3,8,128,2048]{3,1,2,0:T(8,128)(2,1)} %bitcast.247) | data formatting | bytes 25165824
  379.8 5.3 all-to-all-start
  433.9 151.1 %psum.7 = f32[1024]{0:T(1024)} all-reduce(f32[1024]{0:T(1024)S(1)} %get-tuple-element.7), channel_id=1, replica_groups=mesh['seq'=8,'dp'=4] {'seq','dp'}, use_global_device_ids=true, to_apply=%region_11.12 | all-reduce | flops 1024 | bytes 8192 | tf_op jit(solution)/shard_map/psum | solution.py:180
  594.8 11.7 %copy.341 = bf16[3,8,128,2048]{3,1,2,0:T(8,128)(2,1)S(1)} copy(bf16[3,8,128,2048]{3,2,1,0:T(8,128)(2,1)} %bitcast.95) | data formatting | bytes 25165824
  614.2 5.4 copy.316
  (188 shorter events, 169.2 us)
Async XLA Ops:
  7.2 58.3 %copy-start = (bf16[1024,1024]{1,0:T(8,128)(2,1)S(1)}, bf16[1024,1024]{1,0:T(8,128)(2,1)}, u32[]{:S(2)}) copy-start(bf16[1024,1024]{1,0:T(8,128)(2,1)} %param.17) | copy-start | bytes 6291460
  36.5 13.6 %copy-start.13 = (bf16[1,512,1024]{2,1,0:T(8,128)(2,1)S(1)}, bf16[1,512,1024]{2,1,0:T(8,128)(2,1)}, u32[]{:S(2)}) copy-start(bf16[1,512,1024]{2,1,0:T(8,128)(2,1)} %param.11) | copy-start | bytes 3145732
  36.5 13.6 %copy-start.15 = (bf16[1,512,1024]{2,1,0:T(8,128)(2,1)S(1)}, bf16[1,512,1024]{2,1,0:T(8,128)(2,1)}, u32[]{:S(2)}) copy-start(bf16[1,512,1024]{2,1,0:T(8,128)(2,1)} %param.10) | copy-start | bytes 3145732
  45.1 8.9 %copy-start.22 = (bf16[1,512,1024]{2,1,0:T(8,128)(2,1)S(1)}, bf16[1,512,1024]{2,1,0:T(8,128)(2,1)}, u32[]{:S(2)}) copy-start(bf16[1,512,1024]{2,1,0:T(8,128)(2,1)} %param.9) | copy-start | bytes 3145732
  45.1 88.8 %collective-permute-start.1 = (bf16[1,3,128,2048]{3,2,1,0:T(8,128)(2,1)}, bf16[1,3,128,2048]{3,2,1,0:T(8,128)(2,1)}, u32[]{:S(2)}, u32[]{:S(2)}) collective-permute-start(bf16[1,3,128,2048]{3,2,1,0:T(8,128)(2,1)} %get-tuple-element.24), channel_id=1, source_target_pairs={{0,4},{4,0},{8,12},{12,8},{16,20},{20,16},{24,28},{28,24},{1,5},{5... | collective-permute-start | bytes 4718600 | tf_op jit(solution)/shard_map/ppermute | solution.py:145
  45.7 93.6 %collective-permute-start.2 = (bf16[1,3,128,2048]{3,2,1,0:T(8,128)(2,1)}, bf16[1,3,128,2048]{3,2,1,0:T(8,128)(2,1)}, u32[]{:S(2)}, u32[]{:S(2)}) collective-permute-start(bf16[1,3,128,2048]{3,2,1,0:T(8,128)(2,1)} %get-tuple-element.23), channel_id=1, source_target_pairs={{0,8},{4,12},{8,0},{12,4},{16,24},{20,28},{24,16},{28,20},{1,9},{5... | collective-permute-start | bytes 4718600 | tf_op jit(solution)/shard_map/ppermute | solution.py:145
  48.3 97.6 %collective-permute-start.3 = (bf16[1,3,128,2048]{3,2,1,0:T(8,128)(2,1)}, bf16[1,3,128,2048]{3,2,1,0:T(8,128)(2,1)}, u32[]{:S(2)}, u32[]{:S(2)}) collective-permute-start(bf16[1,3,128,2048]{3,2,1,0:T(8,128)(2,1)} %get-tuple-element.22), channel_id=1, source_target_pairs={{0,12},{4,8},{8,4},{12,0},{16,28},{20,24},{24,20},{28,16},{1,13},{... | collective-permute-start | bytes 4718600 | tf_op jit(solution)/shard_map/ppermute | solution.py:145
  48.4 100.3 %collective-permute-start.4 = (bf16[1,3,128,2048]{3,2,1,0:T(8,128)(2,1)}, bf16[1,3,128,2048]{3,2,1,0:T(8,128)(2,1)}, u32[]{:S(2)}, u32[]{:S(2)}) collective-permute-start(bf16[1,3,128,2048]{3,2,1,0:T(8,128)(2,1)} %get-tuple-element.21), channel_id=1, source_target_pairs={{0,16},{4,20},{8,24},{12,28},{16,0},{20,4},{24,8},{28,12},{1,17},{... | collective-permute-start | bytes 4718600 | tf_op jit(solution)/shard_map/ppermute | solution.py:145
  50.9 20.1 %collective-permute-start = (bf16[128,2048]{1,0:T(8,128)(2,1)}, bf16[128,2048]{1,0:T(8,128)(2,1)}, u32[]{:S(2)}, u32[]{:S(2)}) collective-permute-start(bf16[128,2048]{1,0:T(8,128)(2,1)} %fusion.48), channel_id=1, source_target_pairs={{0,4},{4,8},{8,12},{12,16},{16,20},{20,24},{24,28},{1,5},{5,9},{9,... | collective-permute-start | bytes 1572872 | tf_op jit(solution)/shard_map/ppermute | solution.py:16
  68.1 55.4 %copy-start.1 = (s32[1,32]{1,0:T(1,128)S(1)}, s32[1,32]{1,0:T(1,128)}, u32[]{:S(2)}) copy-start(s32[1,32]{1,0:T(1,128)} %param.15) | copy-start | bytes 388
  71.0 154.7 %collective-permute-start.5 = (bf16[1,3,128,2048]{3,2,1,0:T(8,128)(2,1)}, bf16[1,3,128,2048]{3,2,1,0:T(8,128)(2,1)}, u32[]{:S(2)}, u32[]{:S(2)}) collective-permute-start(bf16[1,3,128,2048]{3,2,1,0:T(8,128)(2,1)} %get-tuple-element.20), channel_id=1, source_target_pairs={{0,20},{4,16},{8,28},{12,24},{16,4},{20,0},{24,12},{28,8},{1,21},{... | collective-permute-start | bytes 4718600 | tf_op jit(solution)/shard_map/ppermute | solution.py:145
  133.9 94.5 %collective-permute-start.6 = (bf16[1,3,128,2048]{3,2,1,0:T(8,128)(2,1)}, bf16[1,3,128,2048]{3,2,1,0:T(8,128)(2,1)S(1)}, u32[]{:S(2)}, u32[]{:S(2)}) collective-permute-start(bf16[1,3,128,2048]{3,2,1,0:T(8,128)(2,1)} %get-tuple-element.19), channel_id=1, source_target_pairs={{0,24},{4,28},{8,16},{12,20},{16,8},{20,12},{24,0},{28,4},{1,25},{... | collective-permute-start | bytes 4718600 | tf_op jit(solution)/shard_map/ppermute | solution.py:145
  139.3 90.4 %collective-permute-start.7 = (bf16[1,3,128,2048]{3,2,1,0:T(8,128)(2,1)S(1)}, bf16[1,3,128,2048]{3,2,1,0:T(8,128)(2,1)S(1)}, u32[]{:S(2)}, u32[]{:S(2)}) collective-permute-start(bf16[1,3,128,2048]{3,2,1,0:T(8,128)(2,1)S(1)} %copy-done.29), channel_id=1, source_target_pairs={{0,28},{4,24},{8,20},{12,16},{16,12},{20,8},{24,4},{28,0},{1,29},{... | collective-permute-start | bytes 4718600 | tf_op jit(solution)/shard_map/ppermute | solution.py:145
  261.4 6.1 copy-start.8
  261.7 5.8 copy-start.12
  282.9 4.6 copy-start.2
  282.9 4.6 copy-start.16
  294.9 5.3 copy-start.9
  379.8 215.0 %all-to-all-start = ((bf16[8,3,128,2048]{3,2,1,0:T(8,128)(2,1)}), bf16[8,3,128,2048]{3,2,1,0:T(8,128)(2,1)}, u32[]{:S(2)}, u32[]{:S(2)}) async-start(bf16[8,3,128,2048]{3,2,1,0:T(8,128)(2,1)} %bitcast.250), calls=%async_computation | async-start | bytes 25165824 | tf_op jit(solution)/shard_map/all_to_all | solution.py:205
  385.2 243.7 %reduce-scatter.2.cloned.1.call-start = ((), (), s32[]{:S(2)}) async-start(), calls=%async_computation.2 | async-start | bytes 4325376 | tf_op jit(solution)/shard_map/reduce_scatter | solution.py:170
  411.8 3.8 copy-start.11
  411.8 4.2 copy-start.5
  414.0 205.6 %collective-permute-start.8 = (bf16[128,2048]{0,1:T(8,128)(2,1)}, bf16[128,2048]{0,1:T(8,128)(2,1)}, u32[]{:S(2)}, u32[]{:S(2)}) collective-permute-start(bf16[128,2048]{0,1:T(8,128)(2,1)} %slice_bitcast_fusion), channel_id=1, source_target_pairs={{4,0},{8,4},{12,8},{16,12},{20,16},{24,20},{28,24},{5,1},{9,5},{13... | collective-permute-start | bytes 1572872 | tf_op jit(solution)/shard_map/ppermute | solution.py:16
  422.1 3.7 copy-start.18
  (25 other events, 57.4 us)
Sparse Core Ops, SparseCore 0:
  399.6 151.2 reduce-scatter.1
